TPU v7x, 32 devices: a whole 2x2x4 slice. The times are simulated.
32 devices in a mesh: dp: 8 (over y, x, core), tensor: 4 (over z).
Axes of the slice: x: 2, y: 2, z: 4, core: 2. Of those that a mesh axis runs over, the one named last changes fastest.
Arguments:
- layer_input: bfloat16 [4096, 8192], P('dp', 'tensor'), may hold values from -180 to 180
- gain: bfloat16 [8192], P('tensor'), may hold values from 0.25 to 1.75
- w_kv: bfloat16 [2048, 8192], P(None, 'tensor'), may hold values from -0.125 to 0.125
- d_kv: bfloat16 [4096, 2048], P('dp', 'tensor'), may hold values from -12 to 12
- destination: int32 [4096], P('dp'), may hold values from -1 to 7, as said below
Outputs:
- grad_x: bfloat16 [4096, 8192], P('dp', 'tensor')
- grad_weight: float32 [2048, 8192], P('dp', 'tensor')
Inputs may be any that keep to these rules, and one draw needn't show every extreme that they name: The rows of one device with destination >= 0 are its first rows, 128 of them or more, and some device has no padding. At most 64 rows of one device name the same destination, and some destination is named by exactly 64 rows of every device.
All inputs are finite; a program needn't handle non-finite values.
Results may differ from a plain program's by a relative error of at most 0.0031.
Values may be sent and summed in bfloat16 or wider, within the bound.
A program may use at most 64 MiB of HBM per device.

v0:
```python
import jax
import jax.numpy as jnp
from jax import lax
from jax.sharding import PartitionSpec as P

D = 8192


EPS = 1e-06


def gather_columns(own_cot):
    return lax.all_gather(own_cot, "tensor", axis=1, tiled=True)


def layer_backward(inputs, cotangent, gain, w_kv):
    values = inputs.astype(jnp.float32)
    gain_wide = gain.astype(jnp.float32)
    dnormed = jnp.dot(cotangent, w_kv, preferred_element_type=jnp.float32)
    squares, products = lax.psum(
        (jnp.sum(values * values, axis=1), jnp.sum(values * gain_wide * dnormed, axis=1)), "tensor"
    )
    inverse = lax.rsqrt(squares / D + EPS)
    mean_dot = products / D
    grad_rows = (
        inverse[:, None] * gain_wide * dnormed - values * (inverse**3 * mean_dot)[:, None]
    ).astype(jnp.bfloat16)
    normed = (values * inverse[:, None] * gain_wide).astype(jnp.bfloat16)
    grad_weight = lax.psum_scatter(
        lax.dot_general(
            cotangent, normed, (((0,), (0,)), ((), ())), preferred_element_type=jnp.float32
        ),
        "dp",
        scatter_dimension=0,
        tiled=True,
    )
    return (grad_rows, grad_weight)


def shards(layer_input, gain, w_kv, d_kv, destination):
    dp_count = lax.axis_size("dp")
    row_count = destination.shape[0]
    peer_rows = row_count // dp_count
    peer_ids = jnp.arange(dp_count, dtype=jnp.int32)
    onehot = (destination[:, None] == peer_ids[None, :]).astype(jnp.int32)
    before = jnp.cumsum(onehot, axis=0) - onehot
    slot_rank = jnp.sum(before * onehot, axis=1)
    is_live = destination >= 0
    position = jnp.where(is_live, destination * peer_rows + slot_rank, row_count)
    fetch_row = jnp.minimum(position, row_count - 1)
    outgoing = jnp.zeros_like(layer_input).at[position].set(layer_input, mode="drop")
    incoming = lax.all_to_all(
        outgoing.reshape(dp_count, peer_rows, layer_input.shape[1]),
        "dp",
        split_axis=0,
        concat_axis=0,
        tiled=True,
    ).reshape(row_count, layer_input.shape[1])
    grad_slots, grad_weight = layer_backward(incoming, gather_columns(d_kv), gain, w_kv)
    returned = lax.all_to_all(
        grad_slots.reshape(dp_count, peer_rows, layer_input.shape[1]),
        "dp",
        split_axis=0,
        concat_axis=0,
        tiled=True,
    ).reshape(row_count, layer_input.shape[1])
    grad_x = jnp.where(is_live[:, None], returned[fetch_row], jnp.zeros((), returned.dtype))
    return (grad_x, grad_weight)


def solution(mesh):
    return jax.shard_map(
        shards,
        mesh=mesh,
        in_specs=(P("dp", "tensor"), P("tensor"), P(None, "tensor"), P("dp", "tensor"), P("dp")),
        out_specs=(P("dp", "tensor"), P("dp", "tensor")),
        check_vma=False,
    )
```

profile of v0, /device:TPU:6, one launch (start us, length us, event | category | flops | bytes accessed | tf_op | source)
XLA Modules:
  0.0 213.4 jit_solution(8555713096245465656)
XLA Ops:
  7.2 0.0 all-gather.2.cloned.1.call-start
  7.2 0.7 all-gather.2.cloned.1.call-update
  7.9 0.7 fusion.11
  8.6 1.1 reduce-window.6
  9.7 0.2 slice_reduce_fusion
  10.0 0.8 fusion.10
  10.7 0.7 compare_select_fusion
  11.4 6.1 %scatter_custom_fusion = bf16[512,2048]{1,0:T(8,128)(2,1)} fusion(s32[512]{0:T(512)S(1)} %get-tuple-element.11, bf16[512,2048]{1,0:T(8,128)(2,1)} %param.5, bf16[]{:T(256)} %constant.9.clone.1), kind=kCustom, calls=%fused_computation.15 | custom fusion | bytes 2097664 | tf_op jit(solution)/shard_map/scatter | solution.py:51
  17.6 0.0 copy-start.1
  17.6 4.3 %all-to-all-start = ((bf16[8,64,2048]{2,1,0:T(8,128)(2,1)}), bf16[8,64,2048]{2,1,0:T(8,128)(2,1)S(1)}, u32[]{:S(2)}, u32[]{:S(2)}) async-start(bf16[8,64,2048]{2,1,0:T(8,128)(2,1)} %bitcast.36), calls=%async_computation | async-start | bytes 4194304 | tf_op jit(solution)/shard_map/all_to_all | solution.py:52
  21.9 0.0 reduce-scatter.2.cloned.1.call-start
  21.9 0.0 copy-done.1
  21.9 24.3 %all-to-all-done = bf16[8,64,2048]{2,1,0:T(8,128)(2,1)S(1)} async-done(((bf16[8,64,2048]{2,1,0:T(8,128)(2,1)}), bf16[8,64,2048]{2,1,0:T(8,128)(2,1)S(1)}, u32[]{:S(2)}, u32[]{:S(2)}) %all-to-all-start) | async-done | bytes 2097184 | tf_op jit(solution)/shard_map/all_to_all | solution.py:52
  46.2 0.5 fusion
  46.7 0.1 reduce_sum.31
  46.8 9.9 %all-gather.2.cloned.1.call-done = bf16[512,2048]{1,0:T(8,128)(2,1)} async-done(((bf16[512,512]{1,0:T(8,128)(2,1)}), bf16[512,2048]{1,0:T(8,128)(2,1)}) %all-gather.2.cloned.1.call-update) | async-done | bytes 2097168 | tf_op jit(solution)/shard_map/all_gather | solution.py:13
  56.7 10.5 %fusion.2 = (f32[512]{0:T(512)S(1)}, f32[512,2048]{1,0:T(8,128)}) fusion(bf16[8,64,2048]{2,1,0:T(8,128)(2,1)S(1)} %all-to-all-done, f32[2048]{0:T(1024)S(1)} %convert_element_type.28, bf16[512,2048]{1,0:T(8,128)(2,1)} %all-gather.2.cloned.1.call-done, bf16[2048,2048]{1,0:T(8,128)(2,1)} %param.7), kind=kOutput, calls=%fused_computation.9 | convolution fusion | flops 4299161088 | bytes 16787456 | tf_op jit(solution)/shard_map/dot_general | solution.py:19
  67.2 9.7 %all-reduce = (f32[512]{0:T(512)S(1)}, f32[512]{0:T(512)S(1)}) all-reduce(f32[512]{0:T(512)S(1)} %get-tuple-element.14, f32[512]{0:T(512)S(1)} %reduce_sum.31), channel_id=1, replica_groups=mesh['dp'=8,'tensor'=4] {'tensor'}, use_global_device_ids=true, to_apply=%region_7.8 | all-reduce | flops 1024 | bytes 8192 | tf_op jit(solution)/shard_map/psum | solution.py:20
  76.8 0.0 copy-start.2
  76.8 5.1 %fusion.6 = (bf16[512,2048]{1,0:T(8,128)(2,1)S(1)}, bf16[512,2048]{1,0:T(8,128)(2,1)}) fusion(bf16[8,64,2048]{2,1,0:T(8,128)(2,1)S(1)} %all-to-all-done, f32[2048]{0:T(1024)S(1)} %convert_element_type.28, f32[512]{0:T(512)S(1)} %get-tuple-element.12, f32[512]{0:T(512)S(1)} %get-tuple-element.13, f32[512,2048]{1,0:T(8,128)} %get-tuple-element.15), kind=kLoop, calls=%fused_computation.13 | loop fusion | flops 9437184 | bytes 10498048 | tf_op jit(solution)/shard_map/convert_element_type | solution.py:28
  81.9 0.0 copy-done.2
  81.9 8.1 %convolution_bitcast_fusion = f32[2048,2048]{0,1:T(8,128)} fusion(bf16[512,2048]{1,0:T(8,128)(2,1)S(1)} %get-tuple-element.8, bf16[512,2048]{1,0:T(8,128)(2,1)S(1)} %copy-done.2), kind=kOutput, calls=%fused_computation.2 | convolution fusion | flops 4294967296 | bytes 20971520 | tf_op jit(solution)/shard_map/dot_general | solution.py:30
  90.0 0.0 reduce-scatter.2.cloned.1.call-update
  90.0 0.0 copy-start
  90.0 4.2 %all-to-all-start.1 = ((bf16[8,64,2048]{2,1,0:T(8,128)(2,1)}), bf16[8,64,2048]{2,1,0:T(8,128)(2,1)S(1)}, u32[]{:S(2)}, u32[]{:S(2)}) async-start(bf16[8,64,2048]{2,1,0:T(8,128)(2,1)} %bitcast.37), calls=%async_computation.1 | async-start | bytes 4194304 | tf_op jit(solution)/shard_map/all_to_all | solution.py:60
  94.3 0.0 copy-done
  94.3 24.3 %all-to-all-done.1 = bf16[8,64,2048]{2,1,0:T(8,128)(2,1)S(1)} async-done(((bf16[8,64,2048]{2,1,0:T(8,128)(2,1)}), bf16[8,64,2048]{2,1,0:T(8,128)(2,1)S(1)}, u32[]{:S(2)}, u32[]{:S(2)}) %all-to-all-start.1) | async-done | bytes 2097184 | tf_op jit(solution)/shard_map/all_to_all | solution.py:60
  118.6 3.3 %gather_fusion = bf16[512,2048]{1,0:T(8,128)(2,1)} fusion(bf16[512,2048]{1,0:T(8,128)(2,1)S(1)} %bitcast.35, s32[1024]{0:T(1024)S(1)} %pad_clamp_fusion), kind=kCustom, calls=%fused_computation | custom fusion | bytes 4196352 | tf_op jit(solution)/shard_map/gather | solution.py:67
  121.9 3.1 %broadcast_select_fusion = bf16[512,2048]{1,0:T(8,128)(2,1)} fusion(bf16[512,2048]{1,0:T(8,128)(2,1)} %gather_fusion, pred[512]{0:T(512)(128)(4,1)S(1)} %broadcast_compare_fusion), kind=kLoop, calls=%fused_computation.14 | loop fusion | flops 1048576 | bytes 4194816 | tf_op jit(solution)/shard_map/jit(_where)/select_n | solution.py:67
  125.0 78.7 %reduce-scatter.2.cloned.1.call-done = f32[256,2048]{0,1:T(8,128)} async-done(((f32[2048,2048]{0,1:T(8,128)}), f32[256,2048]{0,1:T(8,128)}) %reduce-scatter.2.cloned.1.call-update) | async-done | bytes 2097168 | tf_op jit(solution)/shard_map/reduce_scatter | solution.py:29
  203.7 2.9 %copy.8 = f32[256,2048]{1,0:T(8,128)} copy(f32[256,2048]{0,1:T(8,128)} %reduce-scatter.2.cloned.1.call-done) | data formatting | bytes 4194304
  (6 shorter events, 0.1 us)
Async XLA Ops:
  7.2 49.5 %all-gather.2.cloned.1.call-start = ((), (), s32[]{:S(2)}) async-start(), calls=%async_computation.3 | async-start | bytes 2621440 | tf_op jit(solution)/shard_map/all_gather | solution.py:13
  17.6 4.3 %copy-start.1 = (bf16[2048]{0:T(1024)(128)(2,1)S(1)}, bf16[2048]{0:T(1024)(128)(2,1)}, u32[]{:S(2)}) copy-start(bf16[2048]{0:T(1024)(128)(2,1)} %param.6) | copy-start | bytes 12292
  17.6 28.7 %all-to-all-start = ((bf16[8,64,2048]{2,1,0:T(8,128)(2,1)}), bf16[8,64,2048]{2,1,0:T(8,128)(2,1)S(1)}, u32[]{:S(2)}, u32[]{:S(2)}) async-start(bf16[8,64,2048]{2,1,0:T(8,128)(2,1)} %bitcast.36), calls=%async_computation | async-start | bytes 4194304 | tf_op jit(solution)/shard_map/all_to_all | solution.py:52
  21.9 181.8 %reduce-scatter.2.cloned.1.call-start = ((), (), s32[]{:S(2)}) async-start(), calls=%async_computation.4 | async-start | bytes 18874368 | tf_op jit(solution)/shard_map/reduce_scatter | solution.py:29
  76.8 5.1 %copy-start.2 = (bf16[512,2048]{1,0:T(8,128)(2,1)S(1)}, bf16[512,2048]{1,0:T(8,128)(2,1)}, u32[]{:S(2)}) copy-start(bf16[512,2048]{1,0:T(8,128)(2,1)} %all-gather.2.cloned.1.call-done) | copy-start | bytes 6291460
  90.0 4.2 %copy-start = (s32[512]{0:T(512)S(1)}, s32[512]{0:T(512)}, u32[]{:S(2)}) copy-start(s32[512]{0:T(512)} %param.9) | copy-start | bytes 6148
  90.0 28.5 %all-to-all-start.1 = ((bf16[8,64,2048]{2,1,0:T(8,128)(2,1)}), bf16[8,64,2048]{2,1,0:T(8,128)(2,1)S(1)}, u32[]{:S(2)}, u32[]{:S(2)}) async-start(bf16[8,64,2048]{2,1,0:T(8,128)(2,1)} %bitcast.37), calls=%async_computation.1 | async-start | bytes 4194304 | tf_op jit(solution)/shard_map/all_to_all | solution.py:60
Sparse Core Ops, SparseCore 0:
  9.6 47.0 all-gather.1
  90.2 113.4 reduce-scatter.1
where the time goes:
time: 216 us; the launch traced here: 213 us
  waiting for transfers between devices  138 us (64%)
  matrix products  18.6 us (9%)
  between operations  14.1 us (7%)
  local copies, waits for them, and re-layouts  12.6 us (6%)
  other arithmetic  12 us (6%)
  blocking collectives  9.67 us (4%)
  starting transfers between devices  8.58 us (4%)
    reduce_scatter x1, waiting for transfers between devices, layer_backward(): lax.psum_scatter(lax.dot_general(cotangent, normed, (((0,), (0,)), ((), (...  78.7 us
    all_to_all x1, waiting for transfers between devices, shards(): lax.all_to_all(outgoing.reshape(dp_count, peer_rows, layer_input.shape[1]...  24.3 us
    all_to_all x1, waiting for transfers between devices, shards(): lax.all_to_all(grad_slots.reshape(dp_count, peer_rows, layer_input.shape[...  24.3 us
    dot_general x1, matrix products, layer_backward(): dnormed = jnp.dot(cotangent, w_kv, preferred_element_type=jnp.float32)  10.5 us
    all_gather x1, waiting for transfers between devices, gather_columns(): return lax.all_gather(own_cot, 'tensor', axis=1, tiled=True)  9.92 us
    psum x1, blocking collectives, layer_backward(): lax.psum((jnp.sum(values * values, axis=1), jnp.sum(values * gain_wide *...  9.67 us
    dot_general x1, matrix products, layer_backward(): lax.dot_general(cotangent, normed, (((0,), (0,)), ((), ())), preferred_el...  8.1 us
    scatter x1, local copies, waits for them, and re-layouts, shards(): jnp.zeros_like(layer_input).at[position].set(layer_input, mode='drop')  6.13 us
  transfers between devices with their start and end apart: 4, of which 4 were waited for; matrix products, arithmetic and copies ran while one was open for 8% of the time, Pallas kernels for 0%

commit v1 on v0

v1 whole, which is shorter than its diff:
```python
import functools

import jax
import jax.numpy as jnp
from jax import lax
from jax.experimental import pallas as pl
from jax.experimental.pallas import tpu as pltpu
from jax.sharding import PartitionSpec as P

D = 8192
EPS = 1e-06
BF = jnp.bfloat16
F32 = jnp.float32


def chip_grid(dp_count):
    chips = dp_count // 2
    width = 1 << ((chips.bit_length() - 1) // 2)
    return chips // width, width


def weight_kernel(height, width, cot_ref, normed_ref, out_ref, rcot, rnormed,
                  sxa, rxa, sya, rya, sxb, rxb, syb, ryb,
                  pair_send, pair_recv, xa_s, xa_r, ya_s, ya_r, xb_s, xb_r, yb_s, yb_r):
    me = lax.axis_index("dp")
    core = lax.rem(me, 2)
    chip = me // 2
    row, col = chip // width, lax.rem(chip, width)
    sibling = me + 1 - 2 * core
    block, features = out_ref.shape
    half = features // 2
    tile = min(256, half)

    def device(r, c):
        return {"dp": (r * width + c) * 2 + core}

    def shift_row(d):
        return lax.rem(row + d, height)

    def shift_col(d):
        return lax.rem(col + d, width)

    barrier = pltpu.get_barrier_semaphore()
    pl.semaphore_signal(barrier, inc=1, device_id={"dp": sibling}, device_id_type=pl.DeviceIdType.MESH)
    for d in range(1, width):
        pl.semaphore_signal(barrier, inc=1, device_id=device(row, shift_col(d)), device_id_type=pl.DeviceIdType.MESH)
    for d in range(1, height):
        pl.semaphore_signal(barrier, inc=1, device_id=device(shift_row(d), col), device_id_type=pl.DeviceIdType.MESH)
    pl.semaphore_wait(barrier, 1 + width - 1 + height - 1)

    def send(src, dst, s, r, dev):
        copy = pltpu.make_async_remote_copy(src_ref=src, dst_ref=dst, send_sem=s, recv_sem=r, device_id=dev,
                                            device_id_type=pl.DeviceIdType.MESH)
        copy.start()
        return copy

    pair = [
        send(cot_ref.at[1 - core], rcot, pair_send.at[0], pair_recv.at[0], {"dp": sibling}),
        send(normed_ref, rnormed, pair_send.at[1], pair_recv.at[1], {"dp": sibling}),
    ]
    for copy in pair:
        copy.wait()

    def product(r, c, first, store):
        index = r * width + c

        def step(i, carry):
            at = pl.ds(pl.multiple_of(i * tile, tile), tile)
            wide = pl.ds(pl.multiple_of(first + i * tile, tile), tile)
            value = jnp.dot(cot_ref[core, index], normed_ref[:, wide], preferred_element_type=F32)
            value += jnp.dot(rcot[index], rnormed[:, wide], preferred_element_type=F32)
            store(at, wide, value)
            return carry

        lax.fori_loop(0, half // tile, step, 0)

    def into(ref):
        def store(at, wide, value):
            ref[:, at] = value.astype(BF)
        return store

    first_x, first_y = {}, {}
    for dr in list(range(1, height)) + [0]:
        for dc in range(1, width):
            product(shift_row(dr), shift_col(dc), 0, into(sxa.at[dc - 1, dr]))
            first_x[dc, dr] = send(sxa.at[dc - 1, dr], rxa.at[dc - 1, dr], xa_s.at[dc - 1, dr], xa_r.at[dc - 1, dr],
                                   device(row, shift_col(dc)))
        if dr > 0:
            for dc in list(range(1, width)):
                product(shift_row(dr), shift_col(dc), half, into(sya.at[dr - 1, dc]))
                first_y[dr, dc] = send(sya.at[dr - 1, dc], rya.at[dr - 1, dc], ya_s.at[dr - 1, dc],
                                       ya_r.at[dr - 1, dc], device(shift_row(dr), col))
    for dr in range(1, height):
        product(shift_row(dr), col, half, into(sya.at[dr - 1, 0]))
        first_y[dr, 0] = send(sya.at[dr - 1, 0], rya.at[dr - 1, 0], ya_s.at[dr - 1, 0], ya_r.at[dr - 1, 0],
                              device(shift_row(dr), col))

    def keep(at, wide, value):
        out_ref[:, wide] = value

    product(row, col, 0, keep)
    product(row, col, half, keep)

    second = []
    for dr in range(1, height):
        for dc in range(1, width):
            first_x[dc, dr].wait_recv()

        def store(at, wide, value, dr=dr):
            for dc in range(1, width):
                value += rxa[dc - 1, dr, :, at].astype(F32)
            syb[dr - 1, :, at] = value.astype(BF)

        product(shift_row(dr), col, 0, store)
        second.append(send(syb.at[dr - 1], ryb.at[dr - 1], yb_s.at[dr - 1], yb_r.at[dr - 1],
                           device(shift_row(dr), col)))
    for dc in range(1, width):
        for dr in range(1, height):
            first_y[dr, dc].wait_recv()

        def store(at, wide, value, dc=dc):
            for dr in range(1, height):
                value += rya[dr - 1, dc, :, at].astype(F32)
            sxb[dc - 1, :, at] = value.astype(BF)

        product(row, shift_col(dc), half, store)
        second.append(send(sxb.at[dc - 1], rxb.at[dc - 1], xb_s.at[dc - 1], xb_r.at[dc - 1],
                           device(row, shift_col(dc))))

    for dc in range(1, width):
        first_x[dc, 0].wait_recv()
    for dr in range(1, height):
        first_y[dr, 0].wait_recv()
    for copy in second:
        copy.wait_recv()

    def finish(i, carry):
        at = pl.ds(pl.multiple_of(i * tile, tile), tile)
        wide = pl.ds(pl.multiple_of(half + i * tile, tile), tile)
        left, right = out_ref[:, at], out_ref[:, wide]
        for dc in range(1, width):
            left += rxa[dc - 1, 0, :, at].astype(F32)
            right += rxb[dc - 1, :, at].astype(F32)
        for dr in range(1, height):
            left += ryb[dr - 1, :, at].astype(F32)
            right += rya[dr - 1, 0, :, at].astype(F32)
        out_ref[:, at] = left
        out_ref[:, wide] = right
        return carry

    lax.fori_loop(0, half // tile, finish, 0)
    for copy in list(first_x.values()) + list(first_y.values()) + second:
        copy.wait_send()


def weight_gradient(dp_count, cot_cores, normed):
    height, width = chip_grid(dp_count)
    cores, chips, block, rows = cot_cores.shape
    features = normed.shape[1]
    half = features // 2
    dma = pltpu.SemaphoreType.DMA
    return pl.pallas_call(
        functools.partial(weight_kernel, height, width),
        out_shape=jax.ShapeDtypeStruct((block, features), F32),
        in_specs=[pl.BlockSpec(memory_space=pltpu.VMEM)] * 2,
        out_specs=pl.BlockSpec(memory_space=pltpu.VMEM),
        scratch_shapes=[
            pltpu.VMEM((chips, block, rows), BF),
            pltpu.VMEM((rows, features), BF),
            pltpu.VMEM((width - 1, height, block, half), BF),
            pltpu.VMEM((width - 1, height, block, half), BF),
            pltpu.VMEM((height - 1, width, block, half), BF),
            pltpu.VMEM((height - 1, width, block, half), BF),
            pltpu.VMEM((width - 1, block, half), BF),
            pltpu.VMEM((width - 1, block, half), BF),
            pltpu.VMEM((height - 1, block, half), BF),
            pltpu.VMEM((height - 1, block, half), BF),
            dma((2,)), dma((2,)),
            dma((width - 1, height)), dma((width - 1, height)),
            dma((height - 1, width)), dma((height - 1, width)),
            dma((width - 1,)), dma((width - 1,)),
            dma((height - 1,)), dma((height - 1,)),
        ],
        compiler_params=pltpu.CompilerParams(collective_id=0, has_side_effects=True,
                                             vmem_limit_bytes=40 * 1024 * 1024),
    )(cot_cores, normed)


def shards(layer_input, gain, w_kv, d_kv, destination):
    dp_count = lax.axis_size("dp")
    row_count = destination.shape[0]
    peer_rows = row_count // dp_count
    columns = d_kv.shape[1]
    slots = lax.all_to_all(d_kv.reshape(dp_count, peer_rows, columns), "dp", split_axis=0, concat_axis=0,
                           tiled=True).reshape(row_count, columns)
    slots = lax.all_gather(slots, "tensor", axis=1, tiled=True)
    values = layer_input.astype(F32)
    gain_wide = gain.astype(F32)
    squares = lax.psum(jnp.sum(values * values, axis=1), "tensor")
    peer_ids = jnp.arange(dp_count, dtype=jnp.int32)
    onehot = (destination[:, None] == peer_ids[None, :]).astype(jnp.int32)
    before = jnp.cumsum(onehot, axis=0) - onehot
    position = jnp.where(destination >= 0, destination * peer_rows + jnp.sum(before * onehot, axis=1), -1)
    place = (position[:, None] == jnp.arange(row_count, dtype=jnp.int32)[None, :]).astype(BF)
    cot = jnp.dot(place, slots, preferred_element_type=F32).astype(BF)
    inverse = lax.rsqrt(squares / D + EPS)
    normed = (values * inverse[:, None] * gain_wide).astype(BF)
    dnormed = jnp.dot(cot, w_kv, preferred_element_type=F32)
    products = lax.psum(jnp.sum(values * gain_wide * dnormed, axis=1), "tensor")
    grad_x = (inverse[:, None] * gain_wide * dnormed
              - values * (inverse**3 * (products / D))[:, None]).astype(BF)
    total = cot.shape[1]
    block = total // dp_count
    cot_cores = cot.T.reshape(dp_count // 2, 2, block, row_count).transpose(1, 0, 2, 3)
    return (grad_x, weight_gradient(dp_count, cot_cores, normed))


def solution(mesh):
    return jax.shard_map(
        shards,
        mesh=mesh,
        in_specs=(P("dp", "tensor"), P("tensor"), P(None, "tensor"), P("dp", "tensor"), P("dp")),
        out_specs=(P("dp", "tensor"), P("dp", "tensor")),
        check_vma=False,
    )
```

time: 216 us -> 156 us (0.72)
  waiting for transfers between devices: 138 us -> 43.4 us
  Pallas kernels: 0 us -> 45.4 us
  blocking collectives: 9.67 us -> 21.2 us
  starting transfers between devices: 8.58 us -> 0.04 us
  local copies, waits for them, and re-layouts: 12.6 us -> 6.39 us
  matrix products: 18.6 us -> 13.5 us
  other arithmetic: 12 us -> 9.57 us
    reduce_scatter x1 -> x0, waiting for transfers between devices: 78.7 us -> none  [layer_backward(): lax.psum_scatter(lax.dot_general(cotangent, normed, (((0,), (0,)), ((), (...]
    all_to_all x2 -> x0, waiting for transfers between devices: 48.6 us -> none  [the longest x1 24.3 us: shards(): lax.all_to_all(outgoing.reshape(dp_count, peer_rows, layer_input.shape[1]...]
    pallas_call x0 -> x1, Pallas kernels: none -> 45.4 us  [weight_gradient(): pl.pallas_call(functools.partial(weight_kernel, height, width), out_shape...]
    all_gather x1, waiting for transfers between devices: 9.92 us -> 43.4 us  [shards(): slots = lax.all_gather(slots, 'tensor', axis=1, tiled=True)]
    all_to_all x0 -> x1, blocking collectives: none -> 11.7 us  [shards(): lax.all_to_all(d_kv.reshape(dp_count, peer_rows, columns), 'dp', split_ax...]
    all_to_all x2 -> x0, starting transfers between devices: 8.54 us -> none  [the longest x1 4.33 us: shards(): lax.all_to_all(outgoing.reshape(dp_count, peer_rows, layer_input.shape[1]...]
    scatter x1 -> x0, local copies, waits for them, and re-layouts: 6.13 us -> none  [shards(): jnp.zeros_like(layer_input).at[position].set(layer_input, mode='drop')]
    dot_general x2, matrix products: 18.6 us -> 13.5 us  [the longest x1 10.6 us: shards(): dnormed = jnp.dot(cot, w_kv, preferred_element_type=F32)]
  transfers between devices with their start and end apart: 4 -> 1, of which waited for: 4 -> 1; matrix products, arithmetic and copies ran while one was open for 8% -> 3% of each run, Pallas kernels for 0% -> 0%
where the time goes in v1:
time: 156 us; the launch traced here: 154 us
  Pallas kernels  45.4 us (29%)
  waiting for transfers between devices  43.4 us (28%)
  blocking collectives  21.2 us (14%)
  between operations  14.1 us (9%)
  matrix products  13.5 us (9%)
  other arithmetic  9.57 us (6%)
  local copies, waits for them, and re-layouts  6.39 us (4%)
    pallas_call x1, Pallas kernels, weight_gradient(): pl.pallas_call(functools.partial(weight_kernel, height, width), out_shape...  45.4 us
    all_gather x1, waiting for transfers between devices, shards(): slots = lax.all_gather(slots, 'tensor', axis=1, tiled=True)  43.4 us
    all_to_all x1, blocking collectives, shards(): lax.all_to_all(d_kv.reshape(dp_count, peer_rows, columns), 'dp', split_ax...  11.7 us
    dot_general x1, matrix products, shards(): dnormed = jnp.dot(cot, w_kv, preferred_element_type=F32)  10.6 us
    psum x1, blocking collectives, shards(): products = lax.psum(jnp.sum(values * gain_wide * dnormed, axis=1), 'tensor')  9.49 us
    convert_element_type x1, other arithmetic, shards(): normed = (values * inverse[:, None] * gain_wide).astype(BF)  5.55 us
  transfers between devices with their start and end apart: 1, of which 1 were waited for; matrix products, arithmetic and copies ran while one was open for 3% of the time, Pallas kernels for 0%

profile of v1, /device:TPU:6, one launch (start us, length us, event | category | flops | bytes accessed | tf_op | source)
XLA Modules:
  0.0 153.5 jit_solution(8502514529495964838)
XLA Ops:
  7.2 0.0 all-gather.2.cloned.1.call-start
  7.2 11.7 %all_to_all.5 = bf16[8,64,512]{2,1,0:T(8,128)(2,1)} all-to-all(bf16[8,64,512]{2,1,0:T(8,128)(2,1)} %bitcast.23), channel_id=1, replica_groups=mesh['dp'=8,'tensor'=4] {'dp'}, dimensions={0} | all-to-all | bytes 1048576 | tf_op jit(solution)/shard_map/all_to_all | solution.py:194
  18.9 0.0 all-gather.2.cloned.1.call-update
  18.9 0.7 convert_element_type.28
  19.6 0.7 fusion.10
  20.3 1.1 reduce-window.6
  21.4 0.2 slice_reduce_fusion
  21.7 0.8 fusion.9
  22.5 0.7 add_select_fusion
  23.2 43.4 %all-gather.2.cloned.1.call-done = bf16[512,2048]{1,0:T(8,128)(2,1)} async-done(((bf16[512,512]{1,0:T(8,128)(2,1)}), bf16[512,2048]{1,0:T(8,128)(2,1)}) %all-gather.2.cloned.1.call-update) | async-done | bytes 2097168 | tf_op jit(solution)/shard_map/all_gather | solution.py:196
  66.5 2.9 %convolution_convert_fusion = bf16[512,2048]{1,0:T(8,128)(2,1)S(1)} fusion(bf16[512,2048]{1,0:T(8,128)(2,1)} %all-gather.2.cloned.1.call-done, s32[512]{0:T(512)S(1)} %add_select_fusion), kind=kOutput, calls=%fused_computation.11 | convolution fusion | flops 1075052544 | bytes 4196352 | tf_op jit(solution)/shard_map/dot_general | solution.py:205
  69.4 0.0 copy-start
  69.4 2.6 %copy.7 = bf16[2048,512]{1,0:T(8,128)(2,1)} copy(bf16[2048,512]{0,1:T(8,128)(2,1)S(1)} %bitcast.21) | data formatting | bytes 4194304 | tf_op jit(solution)/shard_map/convert_element_type | solution.py:205
  72.1 0.0 copy-done
  72.1 0.0 copy-start.1
  72.1 2.0 %copy.10 = bf16[4,2,256,512]{3,2,0,1:T(8,128)(2,1)S(1)} copy(bf16[4,2,256,512]{3,2,1,0:T(8,128)(2,1)} %bitcast.20) | data formatting | bytes 4194304 | tf_op jit(solution)/shard_map/reshape | solution.py:214
  74.0 0.3 copy-done.1
  74.3 10.6 %fusion = (f32[512]{0:T(512)S(1)}, f32[512]{0:T(512)S(1)}, f32[512,2048]{1,0:T(8,128)}) fusion(bf16[512,2048]{1,0:T(8,128)(2,1)S(1)} %copy-done.1, f32[2048]{0:T(1024)S(1)} %convert_element_type.28, bf16[512,2048]{1,0:T(8,128)(2,1)} %copy-done, bf16[2048,2048]{1,0:T(8,128)(2,1)} %param.7), kind=kOutput, calls=%fused_computation.4 | convolution fusion | flops 4301257728 | bytes 16789504 | tf_op jit(solution)/shard_map/dot_general | solution.py:208
  84.9 9.5 %all-reduce = (f32[512]{0:T(512)S(1)}, f32[512]{0:T(512)S(1)}) all-reduce(f32[512]{0:T(512)S(1)} %get-tuple-element.3, f32[512]{0:T(512)S(1)} %get-tuple-element.2), channel_id=1, replica_groups=mesh['dp'=8,'tensor'=4] {'tensor'}, use_global_device_ids=true, to_apply=%region_6.7 | all-reduce | flops 1024 | bytes 8192 | tf_op jit(solution)/shard_map/psum | solution.py:209
  94.4 5.6 %fusion.6 = (bf16[512,2048]{1,0:T(8,128)(2,1)S(1)}, bf16[512,2048]{1,0:T(8,128)(2,1)}) fusion(bf16[512,2048]{1,0:T(8,128)(2,1)} %param.5, f32[2048]{0:T(1024)S(1)} %convert_element_type.28, f32[512]{0:T(512)S(1)} %get-tuple-element.8, f32[512]{0:T(512)S(1)} %get-tuple-element.9, f32[512,2048]{1,0:T(8,128)} %get-tuple-element.10), kind=kLoop, calls=%fused_computation.10 | loop fusion | flops 9437184 | bytes 10498048 | tf_op jit(solution)/shard_map/convert_element_type | solution.py:207
  100.0 45.4 %shard_map.68 = f32[256,2048]{1,0:T(8,128)S(1)} custom-call(bf16[2,4,256,512]{3,2,1,0:T(8,128)(2,1)S(1)} %bitcast.19, bf16[512,2048]{1,0:T(8,128)(2,1)S(1)} %get-tuple-element.6.normed_ref), custom_call_target="tpu_custom_call" | custom-call | tf_op jit(solution)/shard_map/pallas_call | solution.py:162
  145.3 1.3 copy.12
  (3 shorter events, 0.1 us)
Async XLA Ops:
  7.2 59.4 %all-gather.2.cloned.1.call-start = ((), (), s32[]{:S(2)}) async-start(), calls=%async_computation.1 | async-start | bytes 2621440 | tf_op jit(solution)/shard_map/all_gather | solution.py:196
  69.4 2.6 %copy-start = (bf16[512,2048]{1,0:T(8,128)(2,1)}, bf16[512,2048]{1,0:T(8,128)(2,1)S(1)}, u32[]{:S(2)}) copy-start(bf16[512,2048]{1,0:T(8,128)(2,1)S(1)} %convolution_convert_fusion) | copy-start | bytes 6291460
  72.1 2.2 %copy-start.1 = (bf16[512,2048]{1,0:T(8,128)(2,1)S(1)}, bf16[512,2048]{1,0:T(8,128)(2,1)}, u32[]{:S(2)}) copy-start(bf16[512,2048]{1,0:T(8,128)(2,1)} %param.5) | copy-start | bytes 6291460
Sparse Core Ops, SparseCore 0:
  19.1 47.4 all-gather.1

commit v2 on v1

v2 whole, which is shorter than its diff:
```python
import functools

import jax
import jax.numpy as jnp
from jax import lax
from jax.experimental import pallas as pl
from jax.experimental.pallas import tpu as pltpu
from jax.sharding import PartitionSpec as P

D = 8192
EPS = 1e-06
BF = jnp.bfloat16
F32 = jnp.float32


def chip_grid(dp_count):
    chips = dp_count // 2
    width = 1 << ((chips.bit_length() - 1) // 2)
    return chips // width, width


MESH = pl.DeviceIdType.MESH
GROUPS = 4


def kernel(shape, x_hbm, gain_ref, w_hbm, dkv_hbm, dest_ref, gx_hbm, gw_hbm,
           x, w, slots, place, place_t, cot_buf, cot_t, rcot, normed, rnormed, dnormed, gx, total,
           lanes, inv_col, fac_col, sstat, rstat,
           sxa, rxa, sya, rya, sxb, rxb, syb, ryb,
           load_sem, store_sem, own_sem, a2a_s, a2a_r, right_s, right_r, left_s, left_r, stat_s, stat_r,
           pair_s, pair_r, nrm_s, nrm_r, xa_s, xa_r, ya_s, ya_r, xb_s, xb_r, yb_s, yb_r):
    dp_count, depth, height, width = shape
    me = lax.axis_index("dp")
    z = lax.axis_index("tensor")
    core = lax.rem(me, 2)
    chip = me // 2
    row, col = chip // width, lax.rem(chip, width)
    sibling = me + 1 - 2 * core
    rows, features = x.shape
    columns = slots.shape[3]
    peer_rows = slots.shape[2]
    block = total.shape[0]
    half = features // 2
    tile = min(256, half)
    chips_each = (dp_count // 2) // depth
    piece = dp_count // GROUPS

    def remote(src, dst, s, r, dev):
        return pltpu.make_async_remote_copy(src_ref=src, dst_ref=dst, send_sem=s, recv_sem=r, device_id=dev,
                                            device_id_type=MESH)

    def device(r, c):
        return {"dp": (r * width + c) * 2 + core}

    def shift_row(d):
        return lax.rem(row + d, height)

    def shift_col(d):
        return lax.rem(col + d, width)

    load_x = pltpu.make_async_copy(x_hbm, x, load_sem.at[0])
    load_w = pltpu.make_async_copy(w_hbm, w, load_sem.at[1])
    own = pltpu.make_async_copy(dkv_hbm.at[me], slots.at[z, 0], own_sem)
    own.start()
    load_x.start()
    load_w.start()

    barrier = pltpu.get_barrier_semaphore()
    for d in range(1, dp_count):
        pl.semaphore_signal(barrier, inc=1, device_id={"dp": lax.rem(me + d, dp_count)}, device_id_type=MESH)
    for d in range(1, depth):
        pl.semaphore_signal(barrier, inc=1, device_id={"tensor": lax.rem(z + d, depth)}, device_id_type=MESH)
    pl.semaphore_wait(barrier, dp_count - 1 + depth - 1)

    def cot_copy(d):
        peer = lax.rem(me + d, dp_count)
        return remote(dkv_hbm.at[peer], slots.at[z, d], a2a_s.at[d - 1], a2a_r.at[d - 1], {"dp": peer})

    for d in range(1, dp_count):
        cot_copy(d).start()

    def right_copy(step, g):
        ref = slots.at[z - step, pl.ds(g * piece, piece)]
        return remote(ref, ref, right_s.at[step, g], right_r.at[step, g], {"tensor": z + 1})

    def left_copy(step, g):
        ref = slots.at[z + step, pl.ds(g * piece, piece)]
        return remote(ref, ref, left_s.at[step, g], left_r.at[step, g], {"tensor": z - 1})

    def wait_right(step, g):
        ref = slots.at[z - step, pl.ds(g * piece, piece)]
        remote(ref, ref, right_s.at[step, g], right_r.at[step - 1, g], {"tensor": z - 1}).wait_recv()

    def wait_left(step, g):
        ref = slots.at[z + step, pl.ds(g * piece, piece)]
        remote(ref, ref, left_s.at[step, g], left_r.at[step - 1, g], {"tensor": z + 1}).wait_recv()

    for g in range(GROUPS):
        for d in range(g * piece, (g + 1) * piece):
            if d == 0:
                own.wait()
            else:
                cot_copy(d).wait_recv()

        @pl.when(z < depth - 1)
        def _(g=g):
            right_copy(0, g).start()

        @pl.when(z > 0)
        def _(g=g):
            left_copy(0, g).start()

    chunk = 64

    def over_tiles(body, wide):
        def outer(i, carry):
            at = pl.ds(pl.multiple_of(i * chunk, chunk), chunk)

            def inner(j, inner_carry):
                body(at, pl.ds(pl.multiple_of(j * wide, wide), wide))
                return inner_carry

            return lax.fori_loop(0, features // wide, inner, carry)

        lax.fori_loop(0, rows // chunk, outer, 0)

    def row_sums(body, which):
        def outer(i, carry):
            at = pl.ds(pl.multiple_of(i * chunk, chunk), chunk)

            def inner(j, acc):
                return acc + body(at, pl.ds(pl.multiple_of(j * 128, 128), 128))

            lanes[at, :] = lax.fori_loop(0, features // 128, inner, jnp.zeros((chunk, 128), F32), unroll=4)
            return carry

        lax.fori_loop(0, rows // chunk, outer, 0)
        sums = jnp.sum(lanes[...].T, axis=0, keepdims=True)
        sstat[which] = jnp.broadcast_to(sums, (8, rows))
        for d in range(1, depth):
            stat_copy(which, d).start()

    def stat_copy(which, d):
        return remote(sstat.at[which], rstat.at[which, d - 1], stat_s.at[which, d - 1], stat_r.at[which, d - 1],
                      {"tensor": lax.rem(z + d, depth)})

    def row_total(which):
        value = sstat[which]
        for d in range(1, depth):
            stat_copy(which, d).wait_recv()
            value += rstat[which, d - 1]
        return value[0:1, :]

    def as_column(value):
        return jnp.broadcast_to(value, (128, rows)).T

    load_x.wait()

    def square(at, wide):
        values = x[at, wide].astype(F32)
        return values * values

    row_sums(square, 0)

    dest = dest_ref[...]
    dest_col = as_column(dest.astype(F32))[:, 0:1]
    first = lax.broadcasted_iota(jnp.int32, (rows, rows), 0)
    second_axis = lax.broadcasted_iota(jnp.int32, (rows, rows), 1)
    same = (dest_col == dest.astype(F32)) & (first < second_axis)
    rank = jnp.sum(jnp.where(same, 1.0, 0.0), axis=0, keepdims=True)
    offset = me - dest
    offset = jnp.where(offset < 0, offset + dp_count, offset)
    position = jnp.where(dest >= 0, offset.astype(F32) * peer_rows + rank, -1.0)
    place_t[...] = jnp.where(position.astype(jnp.int32) == first, 1.0, 0.0).astype(BF)
    position_col = as_column(position)[:, 0:1].astype(jnp.int32)
    place[...] = jnp.where(position_col == second_axis, 1.0, 0.0).astype(BF)

    def pair_copy(index):
        return remote(cot_t.at[index, 1 - core], rcot.at[index], pair_s.at[index], pair_r.at[index], {"dp": sibling})

    def consume(b, fresh):
        block_slots = slots[b].reshape(rows, columns)
        cot_rows = lax.dot_general(block_slots, place_t[...], (((0,), (0,)), ((), ())),
                                   preferred_element_type=F32).astype(BF)
        for q in range(chips_each):
            for c in range(2):
                start = (q * 2 + c) * block
                cot_t[b * chips_each + q, c] = cot_rows[start:start + block]
            pair_copy(b * chips_each + q).start()
        cot_buf[...] = jnp.dot(place[...], block_slots, preferred_element_type=F32).astype(BF)

        def step(i, carry):
            at = pl.ds(pl.multiple_of(i * tile, tile), tile)
            value = jnp.dot(cot_buf[...], w[b, :, at], preferred_element_type=F32)
            if fresh:
                dnormed[:, at] = value
            else:
                dnormed[:, at] += value
            return carry

        lax.fori_loop(0, features // tile, step, 0)

    def product(index, start, store):
        def step(i, carry):
            at = pl.ds(pl.multiple_of(i * tile, tile), tile)
            wide = pl.ds(pl.multiple_of(start + i * tile, tile), tile)
            value = jnp.dot(cot_t[index, core], normed[:, wide], preferred_element_type=F32)
            value += jnp.dot(rcot[index], rnormed[:, wide], preferred_element_type=F32)
            store(at, wide, value)
            return carry

        lax.fori_loop(0, half // tile, step, 0)

    def xa_copy(dc, dr):
        return remote(sxa.at[dc - 1, dr], rxa.at[dc - 1, dr], xa_s.at[dc - 1, dr], xa_r.at[dc - 1, dr],
                      device(row, shift_col(dc)))

    def ya_copy(dr, dc):
        return remote(sya.at[dr - 1, dc], rya.at[dr - 1, dc], ya_s.at[dr - 1, dc], ya_r.at[dr - 1, dc],
                      device(shift_row(dr), col))

    def xb_copy(dc):
        return remote(sxb.at[dc - 1], rxb.at[dc - 1], xb_s.at[dc - 1], xb_r.at[dc - 1], device(row, shift_col(dc)))

    def yb_copy(dr):
        return remote(syb.at[dr - 1], ryb.at[dr - 1], yb_s.at[dr - 1], yb_r.at[dr - 1], device(shift_row(dr), col))

    def contribute(b):
        for q in range(chips_each):
            index = b * chips_each + q
            dr = lax.rem(index // width - row + height, height)
            dc = lax.rem(lax.rem(index, width) - col + width, width)
            pair_copy(index).wait_recv()

            @pl.when(dc > 0)
            def _():
                def store(at, wide, value):
                    sxa[dc - 1, dr, :, at] = value.astype(BF)

                product(index, 0, store)
                xa_copy(dc, dr).start()

            @pl.when(dr > 0)
            def _():
                def store(at, wide, value):
                    sya[dr - 1, dc, :, at] = value.astype(BF)

                product(index, half, store)
                ya_copy(dr, dc).start()

    load_w.wait()
    consume(z, True)

    inverse = lax.rsqrt(row_total(0) / D + EPS)
    inv_col[...] = as_column(inverse)

    def normalize(at, wide):
        values = x[at, wide].astype(F32)
        normed[at, wide] = (values * inv_col[at, 0:1] * gain_ref[:, wide].astype(F32)).astype(BF)

    wide_tile = min(512, features)
    over_tiles(normalize, wide_tile)
    share = remote(normed, rnormed, nrm_s, nrm_r, {"dp": sibling})
    share.start()

    def chain(step, carry):
        for g in range(GROUPS):
            @pl.when(z - step >= 0)
            def _(g=g):
                wait_right(step, g)

                @pl.when(z < depth - 1)
                def _():
                    right_copy(step, g).start()

            @pl.when(z + step <= depth - 1)
            def _(g=g):
                wait_left(step, g)

                @pl.when(z > 0)
                def _():
                    left_copy(step, g).start()

        @pl.when(z - step >= 0)
        def _():
            consume(z - step, False)

        @pl.when(z + step <= depth - 1)
        def _():
            consume(z + step, False)

        @pl.when(step == 1)
        def _():
            share.wait_recv()

        @pl.when(z - step + 1 >= 0)
        def _():
            contribute(z - step + 1)

        @pl.when((step > 1) & (z + step - 1 <= depth - 1))
        def _():
            contribute(z + step - 1)

        return carry

    lax.fori_loop(1, depth, chain, 0)

    @pl.when(z == depth - 1)
    def _():
        contribute(0)

    @pl.when(z == 0)
    def _():
        contribute(depth - 1)

    def dotted(at, wide):
        return x[at, wide].astype(F32) * gain_ref[:, wide].astype(F32) * dnormed[at, wide]

    row_sums(dotted, 1)

    def keep(at, wide, value):
        total[:, wide] = value

    product(chip, 0, keep)
    product(chip, half, keep)

    for dr in range(1, height):
        for dc in range(1, width):
            xa_copy(dc, dr).wait_recv()

        def store(at, wide, value, dr=dr):
            for dc in range(1, width):
                value += rxa[dc - 1, dr, :, at].astype(F32)
            syb[dr - 1, :, at] = value.astype(BF)

        product(shift_row(dr) * width + col, 0, store)
        yb_copy(dr).start()
    for dc in range(1, width):
        for dr in range(1, height):
            ya_copy(dr, dc).wait_recv()

        def store(at, wide, value, dc=dc):
            for dr in range(1, height):
                value += rya[dr - 1, dc, :, at].astype(F32)
            sxb[dc - 1, :, at] = value.astype(BF)

        product(row * width + shift_col(dc), half, store)
        xb_copy(dc).start()

    inverse_row = lax.rsqrt(row_total_done(sstat, rstat, depth) / D + EPS)
    fac_col[...] = as_column(inverse_row**3 * (row_total(1) / D))

    def gradient(at, wide):
        values = x[at, wide].astype(F32)
        gx[at, wide] = (inv_col[at, 0:1] * gain_ref[:, wide].astype(F32) * dnormed[at, wide]
                        - values * fac_col[at, 0:1]).astype(BF)

    over_tiles(gradient, wide_tile)
    store_gx = pltpu.make_async_copy(gx, gx_hbm, store_sem.at[0])
    store_gx.start()

    for dc in range(1, width):
        xa_copy(dc, 0).wait_recv()
        xb_copy(dc).wait_recv()
    for dr in range(1, height):
        ya_copy(dr, 0).wait_recv()
        yb_copy(dr).wait_recv()

    def finish(i, carry):
        at = pl.ds(pl.multiple_of(i * tile, tile), tile)
        wide = pl.ds(pl.multiple_of(half + i * tile, tile), tile)
        left, right = total[:, at], total[:, wide]
        for dc in range(1, width):
            left += rxa[dc - 1, 0, :, at].astype(F32)
            right += rxb[dc - 1, :, at].astype(F32)
        for dr in range(1, height):
            left += ryb[dr - 1, :, at].astype(F32)
            right += rya[dr - 1, 0, :, at].astype(F32)
        total[:, at] = left
        total[:, wide] = right
        return carry

    lax.fori_loop(0, half // tile, finish, 0)
    store_gw = pltpu.make_async_copy(total, gw_hbm, store_sem.at[1])
    store_gw.start()

    for d in range(1, dp_count):
        cot_copy(d).wait_send()
    for which in range(2):
        for d in range(1, depth):
            stat_copy(which, d).wait_send()

    def drain(step, carry):
        for g in range(GROUPS):
            @pl.when((z - step >= 0) & (z < depth - 1))
            def _(g=g):
                right_copy(step, g).wait_send()

            @pl.when((z + step <= depth - 1) & (z > 0))
            def _(g=g):
                left_copy(step, g).wait_send()

        return carry

    lax.fori_loop(0, depth, drain, 0)
    share.wait_send()
    for index in range(dp_count // 2):
        pair_copy(index).wait_send()
    for dc in range(1, width):
        for dr in range(height):
            xa_copy(dc, dr).wait_send()
        xb_copy(dc).wait_send()
    for dr in range(1, height):
        for dc in range(width):
            ya_copy(dr, dc).wait_send()
        yb_copy(dr).wait_send()
    store_gx.wait()
    store_gw.wait()


def row_total_done(sstat, rstat, depth):
    value = sstat[0]
    for d in range(1, depth):
        value += rstat[0, d - 1]
    return value[0:1, :]


def shards(layer_input, gain, w_kv, d_kv, destination):
    dp_count, depth = lax.axis_size("dp"), lax.axis_size("tensor")
    height, width = chip_grid(dp_count)
    rows, features = layer_input.shape
    columns = d_kv.shape[1]
    chips = dp_count // 2
    block = w_kv.shape[0] // dp_count
    half = features // 2
    dma, vmem = pltpu.SemaphoreType.DMA, pltpu.VMEM
    anywhere = pl.BlockSpec(memory_space=pl.ANY)
    inside = pl.BlockSpec(memory_space=pltpu.VMEM)
    return pl.pallas_call(
        functools.partial(kernel, (dp_count, depth, height, width)),
        out_shape=(jax.ShapeDtypeStruct((rows, features), BF), jax.ShapeDtypeStruct((block, features), F32)),
        in_specs=[anywhere, inside, anywhere, anywhere, inside],
        out_specs=(anywhere, anywhere),
        scratch_shapes=[
            vmem((rows, features), BF),
            vmem((depth, columns, features), BF),
            vmem((depth, dp_count, rows // dp_count, columns), BF),
            vmem((rows, rows), BF),
            vmem((rows, rows), BF),
            vmem((rows, columns), BF),
            vmem((chips, 2, block, rows), BF),
            vmem((chips, block, rows), BF),
            vmem((rows, features), BF),
            vmem((rows, features), BF),
            vmem((rows, features), F32),
            vmem((rows, features), BF),
            vmem((block, features), F32),
            vmem((rows, 128), F32),
            vmem((rows, 128), F32),
            vmem((rows, 128), F32),
            vmem((2, 8, rows), F32),
            vmem((2, depth - 1, 8, rows), F32),
            vmem((width - 1, height, block, half), BF),
            vmem((width - 1, height, block, half), BF),
            vmem((height - 1, width, block, half), BF),
            vmem((height - 1, width, block, half), BF),
            vmem((width - 1, block, half), BF),
            vmem((width - 1, block, half), BF),
            vmem((height - 1, block, half), BF),
            vmem((height - 1, block, half), BF),
            dma((2,)), dma((2,)), dma,
            dma((dp_count - 1,)), dma((dp_count - 1,)),
            dma((depth, GROUPS)), dma((depth, GROUPS)), dma((depth, GROUPS)), dma((depth, GROUPS)),
            dma((2, depth - 1)), dma((2, depth - 1)),
            dma((chips,)), dma((chips,)), dma, dma,
            dma((width - 1, height)), dma((width - 1, height)),
            dma((height - 1, width)), dma((height - 1, width)),
            dma((width - 1,)), dma((width - 1,)),
            dma((height - 1,)), dma((height - 1,)),
        ],
        compiler_params=pltpu.CompilerParams(collective_id=0, has_side_effects=True,
                                             vmem_limit_bytes=56 * 1024 * 1024),
    )(layer_input, gain.reshape(1, features), w_kv.reshape(depth, columns, features),
      d_kv.reshape(dp_count, rows // dp_count, columns), destination.reshape(1, rows))


def solution(mesh):
    return jax.shard_map(
        shards,
        mesh=mesh,
        in_specs=(P("dp", "tensor"), P("tensor"), P(None, "tensor"), P("dp", "tensor"), P("dp")),
        out_specs=(P("dp", "tensor"), P("dp", "tensor")),
        check_vma=False,
    )
```

time: 156 us -> 99.1 us (0.64); the launches traced: 154 us -> 98.8 us
  Pallas kernels: 45.4 us -> 92.2 us
  waiting for transfers between devices: 43.4 us -> 0 us
  blocking collectives: 21.2 us -> 0 us
  matrix products: 13.5 us -> 0 us
  between operations: 14.1 us -> 0.65 us
  other arithmetic: 9.57 us -> 0 us
    pallas_call x1, Pallas kernels: 45.4 us -> 92.2 us  [shards(): pl.pallas_call(functools.partial(kernel, (dp_count, depth, height, width)...]
    all_gather x1 -> x0, waiting for transfers between devices: 43.4 us -> none  [shards(): slots = lax.all_gather(slots, 'tensor', axis=1, tiled=True)]
    dot_general x2 -> x0, matrix products: 13.5 us -> none  [the longest x1 10.6 us: shards(): dnormed = jnp.dot(cot, w_kv, preferred_element_type=F32)]
    all_to_all x1 -> x0, blocking collectives: 11.7 us -> none  [shards(): lax.all_to_all(d_kv.reshape(dp_count, peer_rows, columns), 'dp', split_ax...]
    psum x1 -> x0, blocking collectives: 9.49 us -> none  [shards(): products = lax.psum(jnp.sum(values * gain_wide * dnormed, axis=1), 'tensor')]
    convert_element_type x3 -> x0, other arithmetic: 6.93 us -> none  [the longest x1 5.55 us: shards(): normed = (values * inverse[:, None] * gain_wide).astype(BF)]
    unnamed x5 -> x4, local copies, waits for them, and re-layouts: 1.58 us -> 4.63 us
    convert_element_type x1 -> x0, local copies, waits for them, and re-layouts: 2.63 us -> none  [shards(): cot = jnp.dot(place, slots, preferred_element_type=F32).astype(BF)]
  transfers between devices with their start and end apart: 1 -> 0, of which waited for: 1 -> 0; matrix products, arithmetic and copies ran while one was open for 3% -> 0% of each run, Pallas kernels for 0% -> 0%
where the time goes in v2:
time: 99.1 us; the launch traced here: 98.8 us
  Pallas kernels  92.2 us (93%)
  local copies, waits for them, and re-layouts  5.92 us (6%)
    pallas_call x1, Pallas kernels, shards(): pl.pallas_call(functools.partial(kernel, (dp_count, depth, height, width)...  92.2 us
    unnamed x4, local copies, waits for them, and re-layouts  4.63 us

profile of v2, /device:TPU:6, one launch (start us, length us, event | category | flops | bytes accessed | tf_op | source)
XLA Modules:
  0.0 98.8 jit_solution(14559888203356055705)
XLA Ops:
  0.6 1.3 %reshape.16.gain_ref = bf16[1,2048]{1,0:T(2,128)(2,1)} reshape(bf16[2048]{0:T(1024)(128)(2,1)} %param.6) | data formatting | bytes 8192 | tf_op jit(solution)/shard_map/reshape | solution.py:483
  1.9 92.2 %shard_map.68 = (bf16[512,2048]{1,0:T(8,128)(2,1)}, f32[256,2048]{1,0:T(8,128)}) custom-call(bf16[512,2048]{1,0:T(8,128)(2,1)} %x_hbm.1, bf16[1,2048]{1,0:T(2,128)(2,1)} %reshape.16.gain_ref, bf16[4,512,2048]{2,1,0:T(8,128)(2,1)} %bitcast.3, bf16[8,64,512]{2,1,0:T(8,128)(2,1)} %bitcast.4, s32[1,512]{1,0:T(1,128)} %bitcast.5), custom_call_target="tpu_custom_call" | custom-call | tf_op jit(solution)/shard_map/pallas_call | solution.py:439
  94.2 0.0 copy-start
  94.2 3.3 %copy.9 = bf16[512,2048]{1,0:T(8,128)(2,1)} copy(bf16[512,2048]{1,0:T(8,128)(2,1)} %get-tuple-element.4) | data formatting | bytes 4194304
  97.5 0.0 copy-done
  97.5 1.3 %copy.10 = f32[256,2048]{1,0:T(8,128)} copy(f32[256,2048]{1,0:T(8,128)S(1)} %copy-done) | data formatting | bytes 4194304
Async XLA Ops:
  94.2 3.3 %copy-start = (f32[256,2048]{1,0:T(8,128)S(1)}, f32[256,2048]{1,0:T(8,128)}, u32[]{:S(2)}) copy-start(f32[256,2048]{1,0:T(8,128)} %get-tuple-element.5) | copy-start | bytes 6291460

commit v3 on v2

v3 whole, which is shorter than its diff:
```python
import functools

import jax
import jax.numpy as jnp
from jax import lax
from jax.experimental import pallas as pl
from jax.experimental.pallas import tpu as pltpu
from jax.sharding import PartitionSpec as P

D = 8192
EPS = 1e-06
BF = jnp.bfloat16
F32 = jnp.float32


def chip_grid(dp_count):
    chips = dp_count // 2
    width = 1 << ((chips.bit_length() - 1) // 2)
    return chips // width, width


MESH = pl.DeviceIdType.MESH
LANES = 128


def kernel(shape, x_hbm, gain_ref, w_hbm, dkv_hbm, dest_ref, gx_hbm, gw_hbm,
           x, w, slots, place, place_t, cot_buf, cot_t, rcot, normed, rnormed, dnormed, gx, total,
           lanes, inv_col, fac_col, sstat, rstat,
           sxa, rxa, sya, rya, sxb, rxb, syb, ryb,
           load_sem, load_w_sem, store_sem, own_sem, a2a_s, a2a_r, right_s, right_r, left_s, left_r, stat_s, stat_r,
           pair_s, pair_r, nrm_s, nrm_r, xa_s, xa_r, ya_s, ya_r, xb_s, xb_r, yb_s, yb_r):
    dp_count, depth, height, width = shape
    me = lax.axis_index("dp")
    z = lax.axis_index("tensor")
    core = lax.rem(me, 2)
    chip = me // 2
    row, col = chip // width, lax.rem(chip, width)
    sibling = me + 1 - 2 * core
    rows, features = x.shape
    parts, lists, peer_rows, span = slots.shape[1], slots.shape[2], slots.shape[4], slots.shape[5]
    order = [(h, k) for h in range(parts) for k in range(lists)]
    block = total.shape[0]
    half = features // 2
    tile = min(256, half)
    chips_each = (dp_count // 2) // depth
    part = block // parts
    cut = min(span, block)

    def remote(src, dst, s, r, dev):
        return pltpu.make_async_remote_copy(src_ref=src, dst_ref=dst, send_sem=s, recv_sem=r, device_id=dev,
                                            device_id_type=MESH)

    def device(r, c):
        return {"dp": (r * width + c) * 2 + core}

    def shift_row(d):
        return lax.rem(row + d, height)

    def shift_col(d):
        return lax.rem(col + d, width)

    load_x = pltpu.make_async_copy(x_hbm, x, load_sem)

    def load_w(h, k):
        return pltpu.make_async_copy(w_hbm.at[:, k, h], w.at[:, h, k], load_w_sem.at[h, k])

    def piece_of(peer, h, k):
        return dkv_hbm.at[peer, :, pl.ds((k * parts + h) * span, span)]

    def own_copy(h, k):
        return pltpu.make_async_copy(piece_of(me, h, k), slots.at[z, h, k, 0], own_sem.at[h, k])

    for h, k in order:
        own_copy(h, k).start()
    load_x.start()
    for h, k in order:
        load_w(h, k).start()

    barrier = pltpu.get_barrier_semaphore()
    for d in range(1, dp_count):
        pl.semaphore_signal(barrier, inc=1, device_id={"dp": lax.rem(me + d, dp_count)}, device_id_type=MESH)
    for d in range(1, depth):
        pl.semaphore_signal(barrier, inc=1, device_id={"tensor": lax.rem(z + d, depth)}, device_id_type=MESH)
    pl.semaphore_wait(barrier, dp_count - 1 + depth - 1)

    def cot_copy(d, h, k):
        peer = lax.rem(me + d, dp_count)
        return remote(piece_of(peer, h, k), slots.at[z, h, k, d], a2a_s.at[d - 1, h, k], a2a_r.at[d - 1, h, k],
                      {"dp": peer})

    for h, k in order:
        for d in range(1, dp_count):
            cot_copy(d, h, k).start()

    def right_copy(step, h, k):
        ref = slots.at[z - step, h, k]
        return remote(ref, ref, right_s.at[step, h, k], right_r.at[step, h, k], {"tensor": z + 1})

    def left_copy(step, h, k):
        ref = slots.at[z + step, h, k]
        return remote(ref, ref, left_s.at[step, h, k], left_r.at[step, h, k], {"tensor": z - 1})

    def wait_right(step, h, k):
        ref = slots.at[z - step, h, k]
        remote(ref, ref, right_s.at[step, h, k], right_r.at[step - 1, h, k], {"tensor": z - 1}).wait_recv()

    def wait_left(step, h, k):
        ref = slots.at[z + step, h, k]
        remote(ref, ref, left_s.at[step, h, k], left_r.at[step - 1, h, k], {"tensor": z + 1}).wait_recv()

    for h, k in order:
        own_copy(h, k).wait()
        for d in range(1, dp_count):
            cot_copy(d, h, k).wait_recv()

        @pl.when(z < depth - 1)
        def _(h=h, k=k):
            right_copy(0, h, k).start()

        @pl.when(z > 0)
        def _(h=h, k=k):
            left_copy(0, h, k).start()

    chunk = 64

    def over_tiles(body, wide):
        def outer(i, carry):
            at = pl.ds(pl.multiple_of(i * chunk, chunk), chunk)

            def inner(j, inner_carry):
                body(at, pl.ds(pl.multiple_of(j * wide, wide), wide))
                return inner_carry

            return lax.fori_loop(0, features // wide, inner, carry)

        lax.fori_loop(0, rows // chunk, outer, 0)

    def row_sums(body, which):
        def outer(i, carry):
            at = pl.ds(pl.multiple_of(i * chunk, chunk), chunk)

            def inner(j, acc):
                return acc + body(at, pl.ds(pl.multiple_of(j * 128, 128), 128))

            lanes[at, :] = lax.fori_loop(0, features // 128, inner, jnp.zeros((chunk, 128), F32), unroll=4)
            return carry

        lax.fori_loop(0, rows // chunk, outer, 0)
        sums = jnp.sum(lanes[...].T, axis=0, keepdims=True)
        sstat[which] = jnp.broadcast_to(sums, (8, rows))
        for d in range(1, depth):
            stat_copy(which, d).start()

    def stat_copy(which, d):
        return remote(sstat.at[which], rstat.at[which, d - 1], stat_s.at[which, d - 1], stat_r.at[which, d - 1],
                      {"tensor": lax.rem(z + d, depth)})

    def row_total(which):
        value = sstat[which]
        for d in range(1, depth):
            stat_copy(which, d).wait_recv()
            value += rstat[which, d - 1]
        return value[0:1, :]

    def as_column(value):
        return jnp.broadcast_to(value, (128, rows)).T

    load_x.wait()

    def square(at, wide):
        values = x[at, wide].astype(F32)
        return values * values

    row_sums(square, 0)

    dest = dest_ref[...]
    dest_col = as_column(dest.astype(F32))[:, 0:1]
    first = lax.broadcasted_iota(jnp.int32, (rows, rows), 0)
    second_axis = lax.broadcasted_iota(jnp.int32, (rows, rows), 1)
    same = (dest_col == dest.astype(F32)) & (first < second_axis)
    rank = jnp.sum(jnp.where(same, 1.0, 0.0), axis=0, keepdims=True)
    offset = me - dest
    offset = jnp.where(offset < 0, offset + dp_count, offset)
    position = jnp.where(dest >= 0, offset.astype(F32) * peer_rows + rank, -1.0)
    place_t[...] = jnp.where(position.astype(jnp.int32) == first, 1.0, 0.0).astype(BF)
    position_col = as_column(position)[:, 0:1].astype(jnp.int32)
    place[...] = jnp.where(position_col == second_axis, 1.0, 0.0).astype(BF)

    def pair_copy(index, h):
        at = pl.ds(h * part, part)
        return remote(cot_t.at[index, 1 - core, at], rcot.at[index, at], pair_s.at[index, h], pair_r.at[index, h],
                      {"dp": sibling})

    def rows_of(h):
        if isinstance(h, int):
            return pl.ds(h * part, part)
        return pl.ds(pl.multiple_of(h * part, part), part)

    def consume(b, h, fresh):
        block_slots = jnp.concatenate([slots[b, h, k].reshape(rows, span) for k in range(lists)], axis=1)
        cot_rows = lax.dot_general(block_slots, place_t[...], (((0,), (0,)), ((), ())),
                                   preferred_element_type=F32).astype(BF)
        for k in range(lists):
            for i in range(0, span, cut):
                start = k * parts * span + i
                cot_t[b * chips_each + start // (2 * block), (start // block) % 2,
                      pl.ds(h * span + start % block, cut)] = cot_rows[k * span + i:k * span + i + cut]
        for q in range(chips_each):
            pair_copy(b * chips_each + q, h).start()
        cot_buf[...] = jnp.dot(place[...], block_slots, preferred_element_type=F32).astype(BF)

        def step(i, carry):
            at = pl.ds(pl.multiple_of(i * tile, tile), tile)
            value = jnp.dot(cot_buf[...], w[b, h, :, :, at].reshape(lists * span, tile), preferred_element_type=F32)
            if fresh:
                dnormed[:, at] = value
            else:
                dnormed[:, at] += value
            return carry

        lax.fori_loop(0, features // tile, step, 0)

    def product(index, h, start, store):
        def step(i, carry):
            at = pl.ds(pl.multiple_of(i * tile, tile), tile)
            wide = pl.ds(pl.multiple_of(start + i * tile, tile), tile)
            value = jnp.dot(cot_t[index, core, rows_of(h)], normed[:, wide], preferred_element_type=F32)
            value += jnp.dot(rcot[index, rows_of(h)], rnormed[:, wide], preferred_element_type=F32)
            store(at, wide, value)
            return carry

        lax.fori_loop(0, half // tile, step, 0)

    def xa_copy(dc, dr, h):
        return remote(sxa.at[dc - 1, dr, h], rxa.at[dc - 1, dr, h], xa_s.at[dc - 1, dr, h], xa_r.at[dc - 1, dr, h],
                      device(row, shift_col(dc)))

    def ya_copy(dr, dc, h):
        return remote(sya.at[dr - 1, dc, h], rya.at[dr - 1, dc, h], ya_s.at[dr - 1, dc, h], ya_r.at[dr - 1, dc, h],
                      device(shift_row(dr), col))

    def xb_copy(dc, h):
        return remote(sxb.at[dc - 1, h], rxb.at[dc - 1, h], xb_s.at[dc - 1, h], xb_r.at[dc - 1, h],
                      device(row, shift_col(dc)))

    def yb_copy(dr, h):
        return remote(syb.at[dr - 1, h], ryb.at[dr - 1, h], yb_s.at[dr - 1, h], yb_r.at[dr - 1, h],
                      device(shift_row(dr), col))

    def contribute(b, h):
        for q in range(chips_each):
            index = b * chips_each + q
            dr = lax.rem(index // width - row + height, height)
            dc = lax.rem(lax.rem(index, width) - col + width, width)
            pair_copy(index, h).wait_recv()

            @pl.when(dc > 0)
            def _():
                def store(at, wide, value):
                    sxa[dc - 1, dr, h, :, at] = value.astype(BF)

                product(index, h, 0, store)
                xa_copy(dc, dr, h).start()

            @pl.when(dr > 0)
            def _():
                def store(at, wide, value):
                    sya[dr - 1, dc, h, :, at] = value.astype(BF)

                product(index, h, half, store)
                ya_copy(dr, dc, h).start()

    def second_stage(h):
        for dr in range(1, height):
            for dc in range(1, width):
                xa_copy(dc, dr, h).wait_recv()

            def store(at, wide, value, dr=dr):
                for dc in range(1, width):
                    value += rxa[dc - 1, dr, h, :, at].astype(F32)
                syb[dr - 1, h, :, at] = value.astype(BF)

            product(shift_row(dr) * width + col, h, 0, store)
            yb_copy(dr, h).start()
        for dc in range(1, width):
            for dr in range(1, height):
                ya_copy(dr, dc, h).wait_recv()

            def store(at, wide, value, dc=dc):
                for dr in range(1, height):
                    value += rya[dr - 1, dc, h, :, at].astype(F32)
                sxb[dc - 1, h, :, at] = value.astype(BF)

            product(row * width + shift_col(dc), h, half, store)
            xb_copy(dc, h).start()

    for h, k in order:
        load_w(h, k).wait()
    for h in range(parts):
        consume(z, h, h == 0)

    inverse = lax.rsqrt(row_total(0) / D + EPS)
    inv_col[...] = as_column(inverse)

    def normalize(at, wide):
        values = x[at, wide].astype(F32)
        normed[at, wide] = (values * inv_col[at, 0:1] * gain_ref[:, wide].astype(F32)).astype(BF)

    wide_tile = min(512, features)
    over_tiles(normalize, wide_tile)
    share = remote(normed, rnormed, nrm_s, nrm_r, {"dp": sibling})
    share.start()

    last = parts * (depth - 1) - 1

    def chain(unit, carry):
        h = unit // (depth - 1)
        step = 1 + lax.rem(unit, depth - 1)

        @pl.when(unit == last)
        def _():
            for done in range(parts - 1):
                second_stage(done)

        for k in range(lists):
            @pl.when(z - step >= 0)
            def _(k=k):
                wait_right(step, h, k)

                @pl.when(z < depth - 1)
                def _():
                    right_copy(step, h, k).start()

            @pl.when(z + step <= depth - 1)
            def _(k=k):
                wait_left(step, h, k)

                @pl.when(z > 0)
                def _():
                    left_copy(step, h, k).start()

        @pl.when(z - step >= 0)
        def _():
            consume(z - step, h, False)

        @pl.when(z + step <= depth - 1)
        def _():
            consume(z + step, h, False)

        @pl.when(unit == 0)
        def _():
            share.wait_recv()
            for done in range(parts):
                contribute(z, done)

        @pl.when(z - step >= 0)
        def _():
            contribute(z - step, h)

        @pl.when(z + step <= depth - 1)
        def _():
            contribute(z + step, h)

        return carry

    lax.fori_loop(0, parts * (depth - 1), chain, 0)

    def dotted(at, wide):
        return x[at, wide].astype(F32) * gain_ref[:, wide].astype(F32) * dnormed[at, wide]

    row_sums(dotted, 1)

    for h in range(parts):
        def keep(at, wide, value, h=h):
            total[rows_of(h), wide] = value

        product(chip, h, 0, keep)
        product(chip, h, half, keep)

    second_stage(parts - 1)

    inverse_row = lax.rsqrt(row_total_done(sstat, rstat, depth) / D + EPS)
    fac_col[...] = as_column(inverse_row**3 * (row_total(1) / D))

    def gradient(at, wide):
        values = x[at, wide].astype(F32)
        gx[at, wide] = (inv_col[at, 0:1] * gain_ref[:, wide].astype(F32) * dnormed[at, wide]
                        - values * fac_col[at, 0:1]).astype(BF)

    over_tiles(gradient, wide_tile)
    store_gx = pltpu.make_async_copy(gx, gx_hbm, store_sem.at[0])
    store_gx.start()

    stores = []
    for h in range(parts):
        for dc in range(1, width):
            xa_copy(dc, 0, h).wait_recv()
            xb_copy(dc, h).wait_recv()
        for dr in range(1, height):
            ya_copy(dr, 0, h).wait_recv()
            yb_copy(dr, h).wait_recv()

        def finish(i, carry, h=h):
            at = pl.ds(pl.multiple_of(i * tile, tile), tile)
            wide = pl.ds(pl.multiple_of(half + i * tile, tile), tile)
            left, right = total[rows_of(h), at], total[rows_of(h), wide]
            for dc in range(1, width):
                left += rxa[dc - 1, 0, h, :, at].astype(F32)
                right += rxb[dc - 1, h, :, at].astype(F32)
            for dr in range(1, height):
                left += ryb[dr - 1, h, :, at].astype(F32)
                right += rya[dr - 1, 0, h, :, at].astype(F32)
            total[rows_of(h), at] = left
            total[rows_of(h), wide] = right
            return carry

        lax.fori_loop(0, half // tile, finish, 0)
        store_gw = pltpu.make_async_copy(total.at[rows_of(h)], gw_hbm.at[rows_of(h)], store_sem.at[1 + h])
        store_gw.start()
        stores.append(store_gw)

    for h, k in order:
        for d in range(1, dp_count):
            cot_copy(d, h, k).wait_send()
    for which in range(2):
        for d in range(1, depth):
            stat_copy(which, d).wait_send()

    def drain(step, carry):
        for h, k in order:
            @pl.when((z - step >= 0) & (z < depth - 1))
            def _(h=h, k=k):
                right_copy(step, h, k).wait_send()

            @pl.when((z + step <= depth - 1) & (z > 0))
            def _(h=h, k=k):
                left_copy(step, h, k).wait_send()

        return carry

    lax.fori_loop(0, depth, drain, 0)
    share.wait_send()
    for h in range(parts):
        for index in range(dp_count // 2):
            pair_copy(index, h).wait_send()
        for dc in range(1, width):
            for dr in range(height):
                xa_copy(dc, dr, h).wait_send()
            xb_copy(dc, h).wait_send()
        for dr in range(1, height):
            for dc in range(width):
                ya_copy(dr, dc, h).wait_send()
            yb_copy(dr, h).wait_send()
    store_gx.wait()
    for copy in stores:
        copy.wait()


def row_total_done(sstat, rstat, depth):
    value = sstat[0]
    for d in range(1, depth):
        value += rstat[0, d - 1]
    return value[0:1, :]


def shards(layer_input, gain, w_kv, d_kv, destination):
    dp_count, depth = lax.axis_size("dp"), lax.axis_size("tensor")
    height, width = chip_grid(dp_count)
    rows, features = layer_input.shape
    columns = d_kv.shape[1]
    chips = dp_count // 2
    block = w_kv.shape[0] // dp_count
    half = features // 2
    span = min(LANES, columns)
    parts = max(1, block // span)
    lists = columns // (span * parts)
    part = block // parts
    dma, vmem = pltpu.SemaphoreType.DMA, pltpu.VMEM
    anywhere = pl.BlockSpec(memory_space=pl.ANY)
    inside = pl.BlockSpec(memory_space=pltpu.VMEM)
    return pl.pallas_call(
        functools.partial(kernel, (dp_count, depth, height, width)),
        out_shape=(jax.ShapeDtypeStruct((rows, features), BF), jax.ShapeDtypeStruct((block, features), F32)),
        in_specs=[anywhere, inside, anywhere, anywhere, inside],
        out_specs=(anywhere, anywhere),
        scratch_shapes=[
            vmem((rows, features), BF),
            vmem((depth, parts, lists, span, features), BF),
            vmem((depth, parts, lists, dp_count, rows // dp_count, span), BF),
            vmem((rows, rows), BF),
            vmem((rows, rows), BF),
            vmem((rows, lists * span), BF),
            vmem((chips, 2, block, rows), BF),
            vmem((chips, block, rows), BF),
            vmem((rows, features), BF),
            vmem((rows, features), BF),
            vmem((rows, features), F32),
            vmem((rows, features), BF),
            vmem((block, features), F32),
            vmem((rows, 128), F32),
            vmem((rows, 128), F32),
            vmem((rows, 128), F32),
            vmem((2, 8, rows), F32),
            vmem((2, depth - 1, 8, rows), F32),
            vmem((width - 1, height, parts, part, half), BF),
            vmem((width - 1, height, parts, part, half), BF),
            vmem((height - 1, width, parts, part, half), BF),
            vmem((height - 1, width, parts, part, half), BF),
            vmem((width - 1, parts, part, half), BF),
            vmem((width - 1, parts, part, half), BF),
            vmem((height - 1, parts, part, half), BF),
            vmem((height - 1, parts, part, half), BF),
            dma, dma((parts, lists)), dma((1 + parts,)), dma((parts, lists)),
            dma((dp_count - 1, parts, lists)), dma((dp_count - 1, parts, lists)),
            dma((depth, parts, lists)), dma((depth, parts, lists)),
            dma((depth, parts, lists)), dma((depth, parts, lists)),
            dma((2, depth - 1)), dma((2, depth - 1)),
            dma((chips, parts)), dma((chips, parts)), dma, dma,
            dma((width - 1, height, parts)), dma((width - 1, height, parts)),
            dma((height - 1, width, parts)), dma((height - 1, width, parts)),
            dma((width - 1, parts)), dma((width - 1, parts)),
            dma((height - 1, parts)), dma((height - 1, parts)),
        ],
        compiler_params=pltpu.CompilerParams(collective_id=0, has_side_effects=True,
                                             vmem_limit_bytes=56 * 1024 * 1024),
    )(layer_input, gain.reshape(1, features), w_kv.reshape(depth, lists, parts, span, features),
      d_kv.reshape(dp_count, rows // dp_count, columns), destination.reshape(1, rows))


def solution(mesh):
    return jax.shard_map(
        shards,
        mesh=mesh,
        in_specs=(P("dp", "tensor"), P("tensor"), P(None, "tensor"), P("dp", "tensor"), P("dp")),
        out_specs=(P("dp", "tensor"), P("dp", "tensor")),
        check_vma=False,
    )
```

time: 99.1 us -> 89.1 us (0.90)
  Pallas kernels: 92.2 us -> 81.7 us
    pallas_call x1, Pallas kernels: 92.2 us -> 81.7 us  [shards(): pl.pallas_call(functools.partial(kernel, (dp_count, depth, height, width)...]
where the time goes in v3:
time: 89.1 us; the launch traced here: 88.3 us
  Pallas kernels  81.7 us (92%)
  local copies, waits for them, and re-layouts  5.92 us (7%)
    pallas_call x1, Pallas kernels, shards(): pl.pallas_call(functools.partial(kernel, (dp_count, depth, height, width)...  81.7 us
    unnamed x4, local copies, waits for them, and re-layouts  4.63 us

profile of v3, /device:TPU:6, one launch (start us, length us, event | category | flops | bytes accessed | tf_op | source)
XLA Modules:
  0.0 88.3 jit_solution(7587498755730054586)
XLA Ops:
  0.6 1.3 %reshape.16.gain_ref = bf16[1,2048]{1,0:T(2,128)(2,1)} reshape(bf16[2048]{0:T(1024)(128)(2,1)} %param.6) | data formatting | bytes 8192 | tf_op jit(solution)/shard_map/reshape | solution.py:526
  1.9 81.7 %shard_map.68 = (bf16[512,2048]{1,0:T(8,128)(2,1)}, f32[256,2048]{1,0:T(8,128)}) custom-call(bf16[512,2048]{1,0:T(8,128)(2,1)} %x_hbm.1, bf16[1,2048]{1,0:T(2,128)(2,1)} %reshape.16.gain_ref, bf16[4,2,2,128,2048]{4,3,2,1,0:T(8,128)(2,1)} %bitcast.3, bf16[8,64,512]{2,1,0:T(8,128)(2,1)} %bitcast.4, s32[1,512]{1,0:T(1,128)} %bitcast.5), custom_call_target="tpu_custom_call" | custom-call | tf_op jit(solution)/shard_map/pallas_call | solution.py:481
  83.6 0.0 copy-start
  83.6 3.3 %copy.9 = bf16[512,2048]{1,0:T(8,128)(2,1)} copy(bf16[512,2048]{1,0:T(8,128)(2,1)} %get-tuple-element.4) | data formatting | bytes 4194304
  86.9 0.0 copy-done
  87.0 1.3 %copy.10 = f32[256,2048]{1,0:T(8,128)} copy(f32[256,2048]{1,0:T(8,128)S(1)} %copy-done) | data formatting | bytes 4194304
Async XLA Ops:
  83.6 3.3 %copy-start = (f32[256,2048]{1,0:T(8,128)S(1)}, f32[256,2048]{1,0:T(8,128)}, u32[]{:S(2)}) copy-start(f32[256,2048]{1,0:T(8,128)} %get-tuple-element.5) | copy-start | bytes 6291460

commit v4 on v3

--- a/solution.py
+++ b/solution.py
@@ -25,7 +25,7 @@
 
 def kernel(shape, x_hbm, gain_ref, w_hbm, dkv_hbm, dest_ref, gx_hbm, gw_hbm,
            x, w, slots, place, place_t, cot_buf, cot_t, rcot, normed, rnormed, dnormed, gx, total,
-           lanes, inv_col, fac_col, sstat, rstat,
+           gain_row, lanes, inv_col, fac_col, sstat, rstat,
            sxa, rxa, sya, rya, sxb, rxb, syb, ryb,
            load_sem, load_w_sem, store_sem, own_sem, a2a_s, a2a_r, right_s, right_r, left_s, left_r, stat_s, stat_r,
            pair_s, pair_r, nrm_s, nrm_r, xa_s, xa_r, ya_s, ya_r, xb_s, xb_r, yb_s, yb_r):
@@ -108,18 +108,20 @@
         ref = slots.at[z + step, h, k]
         remote(ref, ref, left_s.at[step, h, k], left_r.at[step - 1, h, k], {"tensor": z + 1}).wait_recv()
 
-    for h, k in order:
+    def launch(h, k):
         own_copy(h, k).wait()
         for d in range(1, dp_count):
             cot_copy(d, h, k).wait_recv()
 
         @pl.when(z < depth - 1)
-        def _(h=h, k=k):
+        def _():
             right_copy(0, h, k).start()
 
         @pl.when(z > 0)
-        def _(h=h, k=k):
+        def _():
             left_copy(0, h, k).start()
+
+    launch(*order[0])
 
     chunk = 64
 
@@ -165,6 +167,7 @@
     def as_column(value):
         return jnp.broadcast_to(value, (128, rows)).T
 
+    gain_row[...] = gain_ref[...].astype(F32).reshape(1, features)
     load_x.wait()
 
     def square(at, wide):
@@ -172,6 +175,8 @@
         return values * values
 
     row_sums(square, 0)
+    for h, k in order[1:2]:
+        launch(h, k)
 
     dest = dest_ref[...]
     dest_col = as_column(dest.astype(F32))[:, 0:1]
@@ -186,6 +191,9 @@
     position_col = as_column(position)[:, 0:1].astype(jnp.int32)
     place[...] = jnp.where(position_col == second_axis, 1.0, 0.0).astype(BF)
 
+    for h, k in order[2:]:
+        launch(h, k)
+
     def pair_copy(index, h):
         at = pl.ds(h * part, part)
         return remote(cot_t.at[index, 1 - core, at], rcot.at[index, at], pair_s.at[index, h], pair_r.at[index, h],
@@ -294,22 +302,20 @@
             product(row * width + shift_col(dc), h, half, store)
             xb_copy(dc, h).start()
 
-    for h, k in order:
-        load_w(h, k).wait()
-    for h in range(parts):
-        consume(z, h, h == 0)
-
     inverse = lax.rsqrt(row_total(0) / D + EPS)
     inv_col[...] = as_column(inverse)
 
     def normalize(at, wide):
         values = x[at, wide].astype(F32)
-        normed[at, wide] = (values * inv_col[at, 0:1] * gain_ref[:, wide].astype(F32)).astype(BF)
+        normed[at, wide] = (values * inv_col[at, 0:1] * gain_row[:, wide]).astype(BF)
 
     wide_tile = min(512, features)
     over_tiles(normalize, wide_tile)
     share = remote(normed, rnormed, nrm_s, nrm_r, {"dp": sibling})
     share.start()
+    for h, k in order:
+        load_w(h, k).wait()
+    consume(z, 0, True)
 
     last = parts * (depth - 1) - 1
 
@@ -339,6 +345,13 @@
                 def _():
                     left_copy(step, h, k).start()
 
+        @pl.when(unit == 0)
+        def _():
+            share.wait_recv()
+            contribute(z, 0)
+            for more in range(1, parts):
+                consume(z, more, False)
+
         @pl.when(z - step >= 0)
         def _():
             consume(z - step, h, False)
@@ -349,9 +362,8 @@
 
         @pl.when(unit == 0)
         def _():
-            share.wait_recv()
-            for done in range(parts):
-                contribute(z, done)
+            for more in range(1, parts):
+                contribute(z, more)
 
         @pl.when(z - step >= 0)
         def _():
@@ -366,7 +378,7 @@
     lax.fori_loop(0, parts * (depth - 1), chain, 0)
 
     def dotted(at, wide):
-        return x[at, wide].astype(F32) * gain_ref[:, wide].astype(F32) * dnormed[at, wide]
+        return x[at, wide].astype(F32) * gain_row[:, wide] * dnormed[at, wide]
 
     row_sums(dotted, 1)
 
@@ -384,7 +396,7 @@
 
     def gradient(at, wide):
         values = x[at, wide].astype(F32)
-        gx[at, wide] = (inv_col[at, 0:1] * gain_ref[:, wide].astype(F32) * dnormed[at, wide]
+        gx[at, wide] = (inv_col[at, 0:1] * gain_row[:, wide] * dnormed[at, wide]
                         - values * fac_col[at, 0:1]).astype(BF)
 
     over_tiles(gradient, wide_tile)
@@ -497,6 +509,7 @@
             vmem((rows, features), F32),
             vmem((rows, features), BF),
             vmem((block, features), F32),
+            vmem((1, features), F32),
             vmem((rows, 128), F32),
             vmem((rows, 128), F32),
             vmem((rows, 128), F32),
@@ -523,7 +536,7 @@
         ],
         compiler_params=pltpu.CompilerParams(collective_id=0, has_side_effects=True,
                                              vmem_limit_bytes=56 * 1024 * 1024),
-    )(layer_input, gain.reshape(1, features), w_kv.reshape(depth, lists, parts, span, features),
+    )(layer_input, gain, w_kv.reshape(depth, lists, parts, span, features),
       d_kv.reshape(dp_count, rows // dp_count, columns), destination.reshape(1, rows))
 
 

time: 89.1 us -> 87.1 us (0.978)
  local copies, waits for them, and re-layouts: 5.92 us -> 4.63 us
  Pallas kernels: 81.7 us -> 80.7 us
    reshape x1 -> x0, local copies, waits for them, and re-layouts: 1.29 us -> none  [shards(): gain.reshape(1, features)]
    pallas_call x1, Pallas kernels: 81.7 us -> 80.7 us  [shards(): pl.pallas_call(functools.partial(kernel, (dp_count, depth, height, width)...]
where the time goes in v4:
time: 87.1 us; the launch traced here: 85.9 us
  Pallas kernels  80.7 us (93%)
  local copies, waits for them, and re-layouts  4.63 us (5%)
    pallas_call x1, Pallas kernels, shards(): pl.pallas_call(functools.partial(kernel, (dp_count, depth, height, width)...  80.7 us
    unnamed x4, local copies, waits for them, and re-layouts  4.63 us

profile of v4, /device:TPU:6, one launch (start us, length us, event | category | flops | bytes accessed | tf_op | source)
XLA Modules:
  0.0 85.9 jit_solution(18355172956566418813)
XLA Ops:
  0.6 80.7 %shard_map.68 = (bf16[512,2048]{1,0:T(8,128)(2,1)}, f32[256,2048]{1,0:T(8,128)}) custom-call(bf16[512,2048]{1,0:T(8,128)(2,1)} %x_hbm.1, bf16[2048]{0:T(1024)(128)(2,1)} %gain_ref.1, bf16[4,2,2,128,2048]{4,3,2,1,0:T(8,128)(2,1)} %bitcast.3, bf16[8,64,512]{2,1,0:T(8,128)(2,1)} %bitcast.4, s32[1,512]{1,0:T(1,128)} %bitcast.5), custom_call_target="tpu_custom_call" | custom-call | tf_op jit(solution)/shard_map/pallas_call | solution.py:493
  81.3 0.0 copy-start
  81.3 3.3 %copy.9 = bf16[512,2048]{1,0:T(8,128)(2,1)} copy(bf16[512,2048]{1,0:T(8,128)(2,1)} %get-tuple-element.4) | data formatting | bytes 4194304
  84.6 0.0 copy-done
  84.6 1.3 %copy.10 = f32[256,2048]{1,0:T(8,128)} copy(f32[256,2048]{1,0:T(8,128)S(1)} %copy-done) | data formatting | bytes 4194304
Async XLA Ops:
  81.3 3.3 %copy-start = (f32[256,2048]{1,0:T(8,128)S(1)}, f32[256,2048]{1,0:T(8,128)}, u32[]{:S(2)}) copy-start(f32[256,2048]{1,0:T(8,128)} %get-tuple-element.5) | copy-start | bytes 6291460
